TPU v7x, 32 devices: a whole 2x2x4 slice. The times are simulated.
32 devices in a mesh: fsdp: 8 (over z, x), ctx: 2 (over core), tp: 2 (over y).
Axes of the slice: x: 2, y: 2, z: 4, core: 2. Of those that a mesh axis runs over, the one named last changes fastest.
Arguments:
- layer_input: bfloat16 [16, 1500, 768], P('fsdp', 'ctx'), may hold values from -6 to 6
- cotangent: bfloat16 [16, 1500, 768], P('fsdp', 'ctx'), may hold values from -6 to 6
- attend_weight: float32 [768, 3, 768], P('fsdp', None, 'tp'), may hold values from -0.3125 to 0.3125
- attend_moment: float32 [768, 3, 768], P('fsdp', None, 'tp'), may hold values from -96 to 96
- attend_square: float32 [768, 3, 768], P('fsdp', None, 'tp'), may hold values from 24 to 96
- shifts_weight: float32 [2, 12, 64], P(None, 'tp', 'fsdp'), may hold values from -1.75 to 1.75
- shifts_moment: float32 [2, 12, 64], P(None, 'tp', 'fsdp'), may hold values from -96 to 96
- shifts_square: float32 [2, 12, 64], P(None, 'tp', 'fsdp'), may hold values from 24 to 96
- output_weight: float32 [768, 768], P('tp', 'fsdp'), may hold values from -1.25 to 1.25
- output_moment: float32 [768, 768], P('tp', 'fsdp'), may hold values from -32 to 32
- output_square: float32 [768, 768], P('tp', 'fsdp'), may hold values from 2.4 to 9.6
- expand_weight: float32 [768, 3072], P('fsdp', 'tp'), may hold values from -0.21875 to 0.21875
- expand_moment: float32 [768, 3072], P('fsdp', 'tp'), may hold values from -32 to 32
- expand_square: float32 [768, 3072], P('fsdp', 'tp'), may hold values from 2.16 to 8.64
- offset_weight: float32 [48, 64], P('tp', 'fsdp'), may hold values from -1.75 to 1.75
- offset_moment: float32 [48, 64], P('tp', 'fsdp'), may hold values from -32 to 32
- offset_square: float32 [48, 64], P('tp', 'fsdp'), may hold values from 2.16 to 8.64
- reduce_weight: float32 [3072, 768], P('tp', 'fsdp'), may hold values from -0.109375 to 0.109375
- reduce_moment: float32 [3072, 768], P('tp', 'fsdp'), may hold values from -64 to 64
- reduce_square: float32 [3072, 768], P('tp', 'fsdp'), may hold values from 8.64 to 34.56
- vectors_weight: float32 [6, 768], P(None, 'fsdp'), may hold values from -0.9 to 1.4
- vectors_moment: float32 [6, 768], P(None, 'fsdp'), may hold values from -96 to 96
- vectors_square: float32 [6, 768], P(None, 'fsdp'), may hold values from 24 to 96
Outputs:
- block_output: bfloat16 [16, 1500, 768], P('fsdp', 'ctx')
- input_grad: float32 [16, 1500, 768], P('fsdp', 'ctx')
- attend_updated: float32 [768, 3, 768], P('fsdp', None, 'tp')
- attend_momentum: float32 [768, 3, 768], P('fsdp', None, 'tp')
- attend_variance: float32 [768, 3, 768], P('fsdp', None, 'tp')
- shifts_updated: float32 [2, 12, 64], P(None, 'tp', 'fsdp')
- shifts_momentum: float32 [2, 12, 64], P(None, 'tp', 'fsdp')
- shifts_variance: float32 [2, 12, 64], P(None, 'tp', 'fsdp')
- output_updated: float32 [768, 768], P('tp', 'fsdp')
- output_momentum: float32 [768, 768], P('tp', 'fsdp')
- output_variance: float32 [768, 768], P('tp', 'fsdp')
- expand_updated: float32 [768, 3072], P('fsdp', 'tp')
- expand_momentum: float32 [768, 3072], P('fsdp', 'tp')
- expand_variance: float32 [768, 3072], P('fsdp', 'tp')
- offset_updated: float32 [48, 64], P('tp', 'fsdp')
- offset_momentum: float32 [48, 64], P('tp', 'fsdp')
- offset_variance: float32 [48, 64], P('tp', 'fsdp')
- reduce_updated: float32 [3072, 768], P('tp', 'fsdp')
- reduce_momentum: float32 [3072, 768], P('tp', 'fsdp')
- reduce_variance: float32 [3072, 768], P('tp', 'fsdp')
- vectors_updated: float32 [6, 768], P(None, 'fsdp')
- vectors_momentum: float32 [6, 768], P(None, 'fsdp')
- vectors_variance: float32 [6, 768], P(None, 'fsdp')
All inputs are finite; a program needn't handle non-finite values.
Results may differ from a plain program's by a relative error of at most 0.014.
The roundings to bfloat16 on the way count: a program that leaves them out, or rounds other values in their place, can miss the bound.
Values may be sent and summed in bfloat16 or wider, within the bound.
No kernel may reach another device: no remote copies, remote signals or barrier semaphores. Data moves between devices by JAX's collectives and lax.ppermute only.
A program may use at most 192 MiB of HBM per device.

v0:
```python
import jax
import jax.numpy as jnp
from jax import lax
from jax.sharding import PartitionSpec as P

HD = 64
STEP = 10


norm_eps = 1e-05
beta_first = 0.9
beta_second = 0.999
adam_eps = 1e-08
rate_matrix = 0.05
rate_vector = 0.5
decay_matrix = 0.01


def layer_norm(values, gain_row, offset_row):
    average = jnp.mean(values, axis=-1, keepdims=True)
    centered = values - average
    variance = jnp.mean(centered * centered, axis=-1, keepdims=True)
    return centered * lax.rsqrt(variance + norm_eps) * gain_row + offset_row


def gelu_exact(values):
    return jax.nn.gelu(values, approximate=False)


def adamw(param, grad, moment, square, rate, decay):
    moment_new = beta_first * moment + (1.0 - beta_first) * grad
    square_new = beta_second * square + (1.0 - beta_second) * grad * grad
    corrected = moment_new / (1.0 - beta_first**STEP)
    normal_sq = square_new / (1.0 - beta_second**STEP)
    param_new = param - rate * (corrected / (jnp.sqrt(normal_sq) + adam_eps) + decay * param)
    return (param_new, moment_new, square_new)


def local(
    layer_input,
    cotangent,
    attend_weight,
    attend_moment,
    attend_square,
    shifts_weight,
    shifts_moment,
    shifts_square,
    output_weight,
    output_moment,
    output_square,
    expand_weight,
    expand_moment,
    expand_square,
    offset_weight,
    offset_moment,
    offset_square,
    reduce_weight,
    reduce_moment,
    reduce_square,
    vectors_weight,
    vectors_moment,
    vectors_square,
):
    bfloat = jnp.bfloat16
    single = jnp.float32
    attend_full, output_full, expand_full, reduce_full, shifts_full, offset_full, vectors_full = (
        lax.all_gather(attend_weight.astype(bfloat), "fsdp", axis=0, tiled=True),
        lax.all_gather(output_weight.astype(bfloat), "fsdp", axis=1, tiled=True),
        lax.all_gather(expand_weight.astype(bfloat), "fsdp", axis=0, tiled=True),
        lax.all_gather(reduce_weight.astype(bfloat), "fsdp", axis=1, tiled=True),
        lax.all_gather(shifts_weight.astype(bfloat), "fsdp", axis=2, tiled=True),
        lax.all_gather(offset_weight.astype(bfloat), "fsdp", axis=1, tiled=True),
        lax.all_gather(vectors_weight.astype(bfloat), "fsdp", axis=1, tiled=True),
    )
    clip_count, row_count, model_width = layer_input.shape
    token_count = clip_count * row_count
    local_width = attend_full.shape[2]
    head_count = local_width // HD
    frames = row_count * lax.axis_size("ctx")
    score_scale = HD ** (-0.5)
    vector_rows = vectors_full.astype(single)
    tokens = layer_input.reshape(token_count, model_width).astype(single)
    normed_one = layer_norm(tokens, vector_rows[0], vector_rows[1]).astype(bfloat)
    project = jnp.dot(
        normed_one, attend_full.reshape(model_width, 3 * local_width), preferred_element_type=single
    )
    project = project.reshape(token_count, 3, local_width)
    shift_rows = shifts_full.astype(single).reshape(2, local_width)
    queries = (
        (project[:, 0] + shift_rows[0]).astype(bfloat).reshape(clip_count, row_count, local_width)
    )
    keys_local = project[:, 1].astype(bfloat).reshape(clip_count, row_count, local_width)
    values_local = (
        (project[:, 2] + shift_rows[1]).astype(bfloat).reshape(clip_count, row_count, local_width)
    )
    keys_all, values_all = (
        lax.all_gather(keys_local, "ctx", axis=1, tiled=True),
        lax.all_gather(values_local, "ctx", axis=1, tiled=True),
    )

    def pick(source, flat_index, length):
        clip_id = flat_index // head_count
        column = flat_index % head_count * HD
        return lax.dynamic_slice(source, (clip_id, 0, column), (1, length, HD))[0]

    def to_rows(per_head, length):
        shaped = per_head.reshape(clip_count, head_count, length, HD).transpose(0, 2, 1, 3)
        return shaped.reshape(clip_count, length, local_width)

    def attend_one(flat_index):
        query_head = pick(queries, flat_index, row_count)
        key_head = pick(keys_all, flat_index, frames)
        value_head = pick(values_all, flat_index, frames)
        scores = (
            jnp.einsum("qd,kd->qk", query_head, key_head, preferred_element_type=single)
            * score_scale
        )
        row_top = jnp.max(scores, axis=1, keepdims=True)
        raised = jnp.exp(scores - row_top)
        row_sum = jnp.sum(raised, axis=1, keepdims=True)
        weights = (raised / row_sum).astype(bfloat)
        return (jnp.dot(weights, value_head, preferred_element_type=single), row_top, row_sum)

    pair_ids = jnp.arange(clip_count * head_count)
    head_out, row_tops, row_sums = lax.map(attend_one, pair_ids)
    attended = to_rows(head_out, row_count).reshape(token_count, local_width).astype(bfloat)
    branch = (
        lax.psum(jnp.dot(attended, output_full, preferred_element_type=single), "tp")
        + vector_rows[2]
    )
    hidden_one = tokens + branch
    normed_two = layer_norm(hidden_one, vector_rows[3], vector_rows[4]).astype(bfloat)
    expanded = jnp.dot(normed_two, expand_full, preferred_element_type=single) + offset_full.astype(
        single
    ).reshape(-1)
    activated = gelu_exact(expanded).astype(bfloat)
    mixed = (
        lax.psum(
            jnp.dot(activated, reduce_full, preferred_element_type=single).astype(jnp.bfloat16),
            "tp",
        ).astype(jnp.float32)
        + vector_rows[5]
    )
    block_output = (hidden_one + mixed).astype(bfloat).reshape(clip_count, row_count, model_width)
    grad_mixed = cotangent.reshape(token_count, model_width)
    grad_reduce = jnp.einsum("nf,nd->fd", activated, grad_mixed, preferred_element_type=single)
    grad_last = jnp.sum(grad_mixed.astype(single), axis=0)
    grad_activated = jnp.einsum("nd,fd->nf", grad_mixed, reduce_full, preferred_element_type=single)
    recomputed, gelu_back = jax.vjp(gelu_exact, expanded)
    grad_expanded = gelu_back(grad_activated)[0].astype(bfloat)
    grad_expand = jnp.einsum("nd,nf->df", normed_two, grad_expanded, preferred_element_type=single)
    grad_offset = jnp.sum(grad_expanded.astype(single), axis=0).reshape(offset_full.shape)
    grad_normed_two = lax.psum(
        jnp.einsum("nf,df->nd", grad_expanded, expand_full, preferred_element_type=single), "tp"
    )
    second_value, second_back = jax.vjp(layer_norm, hidden_one, vector_rows[3], vector_rows[4])
    grad_from_norm, grad_gain_two, grad_shift_two = second_back(grad_normed_two)
    grad_hidden = grad_mixed.astype(single) + grad_from_norm
    grad_branch = grad_hidden.astype(bfloat)
    grad_output = jnp.einsum("nc,nd->cd", attended, grad_branch, preferred_element_type=single)
    grad_bias_out = jnp.sum(grad_branch.astype(single), axis=0)
    grad_attended = jnp.einsum("nd,cd->nc", grad_branch, output_full, preferred_element_type=single)
    grad_attended = grad_attended.astype(bfloat).reshape(clip_count, row_count, local_width)

    def attend_grad(inputs):
        flat_index, row_top, row_sum = inputs
        query_head = pick(queries, flat_index, row_count)
        key_head = pick(keys_all, flat_index, frames)
        value_head = pick(values_all, flat_index, frames)
        grad_head = pick(grad_attended, flat_index, row_count)
        scores = (
            jnp.einsum("qd,kd->qk", query_head, key_head, preferred_element_type=single)
            * score_scale
        )
        weights = jnp.exp(scores - row_top) / row_sum
        grad_weights = jnp.einsum("qd,kd->qk", grad_head, value_head, preferred_element_type=single)
        inner = jnp.sum(weights * grad_weights, axis=1, keepdims=True)
        grad_scores = (weights * (grad_weights - inner) * score_scale).astype(bfloat)
        grad_query = jnp.einsum("qk,kd->qd", grad_scores, key_head, preferred_element_type=single)
        grad_key = jnp.einsum("qk,qd->kd", grad_scores, query_head, preferred_element_type=single)
        grad_value = jnp.einsum(
            "qk,qd->kd", weights.astype(bfloat), grad_head, preferred_element_type=single
        )
        return (grad_query, grad_key, grad_value)

    grad_query, grad_key, grad_value = lax.map(attend_grad, (pair_ids, row_tops, row_sums))
    grad_keys, grad_values = (
        lax.psum_scatter(to_rows(grad_key, frames), "ctx", scatter_dimension=1, tiled=True),
        lax.psum_scatter(to_rows(grad_value, frames), "ctx", scatter_dimension=1, tiled=True),
    )
    grad_project = jnp.stack(
        [
            to_rows(grad_query, row_count).astype(bfloat),
            grad_keys.astype(bfloat),
            grad_values.astype(bfloat),
        ],
        axis=2,
    )
    grad_project = grad_project.reshape(token_count, 3, local_width)
    grad_attend = jnp.einsum("nd,ntc->dtc", normed_one, grad_project, preferred_element_type=single)
    grad_shifts = jnp.sum(grad_project[:, 0::2].astype(single), axis=0).reshape(shifts_full.shape)
    grad_normed_one = lax.psum(
        jnp.einsum("ntc,dtc->nd", grad_project, attend_full, preferred_element_type=single).astype(
            jnp.bfloat16
        ),
        "tp",
    ).astype(jnp.float32)
    first_value, first_back = jax.vjp(layer_norm, tokens, vector_rows[0], vector_rows[1])
    grad_tokens, grad_gain_one, grad_shift_one = first_back(grad_normed_one)
    input_grad = (grad_hidden + grad_tokens).reshape(clip_count, row_count, model_width)
    grad_vectors = jnp.stack(
        [grad_gain_one, grad_shift_one, grad_bias_out, grad_gain_two, grad_shift_two, grad_last]
    )
    (
        owned_attend,
        owned_shifts,
        owned_output,
        owned_expand,
        owned_offset,
        owned_reduce,
        owned_vectors,
    ) = (
        lax.psum_scatter(grad_attend, "fsdp", scatter_dimension=0, tiled=True),
        lax.psum_scatter(grad_shifts, "fsdp", scatter_dimension=2, tiled=True),
        lax.psum_scatter(grad_output, "fsdp", scatter_dimension=1, tiled=True),
        lax.psum_scatter(grad_expand, "fsdp", scatter_dimension=0, tiled=True),
        lax.psum_scatter(grad_offset, "fsdp", scatter_dimension=1, tiled=True),
        lax.psum_scatter(grad_reduce, "fsdp", scatter_dimension=1, tiled=True),
        lax.psum_scatter(grad_vectors, "fsdp", scatter_dimension=1, tiled=True),
    )
    (
        total_attend,
        total_shifts,
        total_output,
        total_expand,
        total_offset,
        total_reduce,
        total_vectors,
    ) = lax.psum(
        (
            owned_attend,
            owned_shifts,
            owned_output,
            owned_expand,
            owned_offset,
            owned_reduce,
            owned_vectors,
        ),
        "ctx",
    )
    attend_new = adamw(
        attend_weight, total_attend, attend_moment, attend_square, rate_matrix, decay_matrix
    )
    shifts_new = adamw(shifts_weight, total_shifts, shifts_moment, shifts_square, rate_vector, 0.0)
    output_new = adamw(
        output_weight, total_output, output_moment, output_square, rate_matrix, decay_matrix
    )
    expand_new = adamw(
        expand_weight, total_expand, expand_moment, expand_square, rate_matrix, decay_matrix
    )
    offset_new = adamw(offset_weight, total_offset, offset_moment, offset_square, rate_vector, 0.0)
    reduce_new = adamw(
        reduce_weight, total_reduce, reduce_moment, reduce_square, rate_matrix, decay_matrix
    )
    vectors_new = adamw(
        vectors_weight, total_vectors, vectors_moment, vectors_square, rate_vector, 0.0
    )
    return (
        block_output,
        input_grad,
        attend_new[0],
        attend_new[1],
        attend_new[2],
        shifts_new[0],
        shifts_new[1],
        shifts_new[2],
        output_new[0],
        output_new[1],
        output_new[2],
        expand_new[0],
        expand_new[1],
        expand_new[2],
        offset_new[0],
        offset_new[1],
        offset_new[2],
        reduce_new[0],
        reduce_new[1],
        reduce_new[2],
        vectors_new[0],
        vectors_new[1],
        vectors_new[2],
    )


def solution(mesh):
    placed = (
        P("fsdp", "ctx", None),
        P("fsdp", "ctx", None),
        P("fsdp", None, "tp"),
        P("fsdp", None, "tp"),
        P("fsdp", None, "tp"),
        P(None, "tp", "fsdp"),
        P(None, "tp", "fsdp"),
        P(None, "tp", "fsdp"),
        P("tp", "fsdp"),
        P("tp", "fsdp"),
        P("tp", "fsdp"),
        P("fsdp", "tp"),
        P("fsdp", "tp"),
        P("fsdp", "tp"),
        P("tp", "fsdp"),
        P("tp", "fsdp"),
        P("tp", "fsdp"),
        P("tp", "fsdp"),
        P("tp", "fsdp"),
        P("tp", "fsdp"),
        P(None, "fsdp"),
        P(None, "fsdp"),
        P(None, "fsdp"),
    )
    return jax.shard_map(
        local,
        mesh=mesh,
        in_specs=placed,
        out_specs=(
            P("fsdp", "ctx", None),
            P("fsdp", "ctx", None),
            P("fsdp", None, "tp"),
            P("fsdp", None, "tp"),
            P("fsdp", None, "tp"),
            P(None, "tp", "fsdp"),
            P(None, "tp", "fsdp"),
            P(None, "tp", "fsdp"),
            P("tp", "fsdp"),
            P("tp", "fsdp"),
            P("tp", "fsdp"),
            P("fsdp", "tp"),
            P("fsdp", "tp"),
            P("fsdp", "tp"),
            P("tp", "fsdp"),
            P("tp", "fsdp"),
            P("tp", "fsdp"),
            P("tp", "fsdp"),
            P("tp", "fsdp"),
            P("tp", "fsdp"),
            P(None, "fsdp"),
            P(None, "fsdp"),
            P(None, "fsdp"),
        ),
        check_vma=False,
    )
```

profile of v0, /device:TPU:0, one launch (start us, length us, event | category | flops | bytes accessed | tf_op | source)
XLA Modules:
  0.0 1500.3 jit_solution(9641253117920323761)
XLA Ops:
  9.9 27.8 %all-gather = bf16[8,96,6]{1,2,0:T(8,128)(2,1)S(1)} all-gather(bf16[1,96,6]{1,2,0:T(8,128)(2,1)S(1)} %convert_bitcast_fusion), channel_id=1, replica_groups=mesh['fsdp'=8,'ctx'=2,'tp'=2] {'fsdp'}, dimensions={0}, use_global_device_ids=true | all-gather | bytes 10368 | tf_op jit(solution)/shard_map/all_gather | solution.py:73
  41.4 10.6 multiply_reduce_fusion.5
  79.7 30.6 %all_gather.29 = bf16[2,6,64]{1,0,2:T(2,128)(2,1)S(1)} all-gather(bf16[2,6,8]{1,0,2:T(2,128)(2,1)S(1)} %copy.166), channel_id=1, replica_groups=mesh['fsdp'=8,'ctx'=2,'tp'=2] {'fsdp'}, dimensions={2}, use_global_device_ids=true | all-gather | bytes 1728 | tf_op jit(solution)/shard_map/all_gather | solution.py:71
  122.7 33.6 %all_gather.32 = bf16[384,768]{0,1:T(8,128)(2,1)} all-gather(bf16[384,96]{0,1:T(8,128)(2,1)S(1)} %convert_element_type.179), channel_id=1, replica_groups=mesh['fsdp'=8,'ctx'=2,'tp'=2] {'fsdp'}, dimensions={1}, use_global_device_ids=true | all-gather | bytes 663552 | tf_op jit(solution)/shard_map/all_gather | solution.py:68
  169.2 107.2 %while.32 = (s32[]{:T(128)}, bf16[12,750,64]{1,2,0:T(8,128)(2,1)}, f32[12,750,1]{1,2,0:T(1,128)}, f32[12,750,1]{1,2,0:T(1,128)}, s32[12]{0:T(128)S(1)}, /*index=...) while((s32[]{:T(128)}, bf16[12,750,64]{1,2,0:T(8,128)(2,1)}, ...), condition=%wide.region_5.6_spmd, body=%wide.region_2.5_spmd.sunk | while | flops 298123520 | bytes 14688748 | solution.py:125
  300.2 26.4 %all_gather.34 = bf16[24,64]{0,1:T(8,128)(2,1)S(1)} all-gather(bf16[24,8]{0,1:T(8,128)(2,1)S(1)} %convert_element_type.182), channel_id=1, replica_groups=mesh['fsdp'=8,'ctx'=2,'tp'=2] {'fsdp'}, dimensions={1}, use_global_device_ids=true | all-gather | bytes 3456 | tf_op jit(solution)/shard_map/all_gather | solution.py:72
  330.6 74.7 %all-reduce.15.cloned.1.call-done = f32[1500,768]{1,0:T(8,128)} async-done(((f32[1500,768]{1,0:T(8,128)}), f32[1500,768]{1,0:T(8,128)}) %all-reduce.15.cloned.1.call-update) | async-done | bytes 4608016 | tf_op jit(solution)/shard_map/psum | solution.py:128
  412.4 47.6 %all-gather.13.cloned.1.call-done = bf16[768,1536]{1,0:T(8,128)(2,1)} async-done(((bf16[96,1536]{1,0:T(8,128)(2,1)}), bf16[768,1536]{1,0:T(8,128)(2,1)}) %all-gather.13.cloned.1.call-update) | async-done | bytes 2359312 | tf_op jit(solution)/shard_map/all_gather | solution.py:69
  460.0 10.7 convolution_add_fusion
  470.7 42.6 %all-gather.15.cloned.1.call-done = bf16[1536,768]{0,1:T(8,128)(2,1)} async-done(((bf16[1536,96]{0,1:T(8,128)(2,1)}), bf16[1536,768]{0,1:T(8,128)(2,1)}) %all-gather.15.cloned.1.call-update) | async-done | bytes 2359312 | tf_op jit(solution)/shard_map/all_gather | solution.py:70
  513.3 27.4 %convert_reduce_fusion = (f32[1536]{0:T(1024)}, bf16[1500,1536]{1,0:T(8,128)(2,1)S(1)}, f32[1500,1536]{1,0:T(8,128)}) fusion(f32[1500,1536]{1,0:T(8,128)} %convolution_add_fusion, bf16[1500,768]{1,0:T(8,128)(2,1)S(1)} %reshape.262, bf16[1536,768]{0,1:T(8,128)(2,1)} %all-gather.15.cloned.1.call-done), kind=kOutput, calls=%fused_computation.53 | convolution fusion | flops 3709438464 | bytes 27709440 | tf_op jit(solution)/shard_map/nd,fd->nf/dot_general | solution.py:148
  542.7 5.4 fusion.87
  550.0 11.5 multiply_convert_fusion.1
  561.5 8.4 convolution_convert_fusion
  570.0 94.0 %all-reduce.17.cloned.1.call-done = f32[1500,768]{1,0:T(8,128)} async-done(((f32[1500,768]{1,0:T(8,128)}), f32[1500,768]{1,0:T(8,128)}) %all-reduce.17.cloned.1.call-update) | async-done | bytes 4608016 | tf_op jit(solution)/shard_map/psum | solution.py:153
  682.4 178.9 %while.33 = (s32[]{:T(128)}, bf16[12,750,64]{1,2,0:T(8,128)(2,1)}, f32[12,1500,64]{1,2,0:T(8,128)}, f32[12,1500,64]{1,2,0:T(8,128)}, s32[12]{0:T(128)S(1)}, /*in...) while((s32[]{:T(128)}, bf16[12,750,64]{1,2,0:T(8,128)(2,1)}, ...), condition=%wide.region_15.16_spmd, body=%wide.region_13.15_spmd.sunk | while | flops 731249280 | bytes 36869316 | solution.py:186
  861.3 8.1 copy.181
  869.3 8.1 copy.179
  877.5 27.6 %all-reduce.22 = (bf16[2,1500,384]{2,0,1:T(2,128)(2,1)}, bf16[2,1500,384]{2,0,1:T(2,128)(2,1)}) all-reduce(f32[2,1500,384]{2,0,1:T(2,128)} %copy.181, f32[2,1500,384]{2,0,1:T(2,128)} %copy.179), channel_id=3, replica_groups=mesh['fsdp'=8,'ctx'=2,'tp'=2] {'ctx'}, use_global_device_ids=true, to_apply=%region_17.18.clone | all-reduce | flops 2304000 | bytes 13824000
  924.8 7.2 bitcast_convert_fusion
  937.9 10.2 fusion.71
  948.2 7.9 fusion.89
  957.4 92.2 %all-reduce.21.cloned.1.call-done = (bf16[1500,768]{1,0:T(8,128)(2,1)}, bf16[1500,768]{1,0:T(8,128)(2,1)}) async-done(((bf16[1500,768]{1,0:T(8,128)(2,1)}, bf16[1500,768]{1,0:T(8,128)(2,1)}), (bf16[1500,768]{1,0:T(8,128)(2,1)}, bf16[1500,768]{1,0:T(8,128)(2,1)})) %all-reduce.21.cloned.1.call-update) | async-done | bytes 4608016 | tf_op jit(solution)/shard_map/psum | solution.py:138
  1054.4 7.9 fusion.50
  1070.5 37.3 %all-reduce.4 = (f32[2,6,64]{2,1,0:T(8,128)S(1)}, f32[24,64]{1,0:T(8,128)S(1)}) all-reduce(f32[2,6,64]{2,1,0:T(8,128)S(1)} %reshape.269, f32[24,64]{1,0:T(8,128)S(1)} %reshape.270), channel_id=5, replica_groups=mesh['fsdp'=8,'ctx'=2,'tp'=2] {'fsdp'}, use_global_device_ids=true, to_apply=%region_24.25.clone | all-reduce | flops 2304 | bytes 18432
  1127.1 87.9 %reduce-scatter.14.cloned.1.call-done = f32[96,1536]{1,0:T(8,128)} async-done(((f32[768,1536]{1,0:T(8,128)}), f32[96,1536]{1,0:T(8,128)}) %reduce-scatter.14.cloned.1.call-update) | async-done | bytes 589840 | tf_op jit(solution)/shard_map/reduce_scatter | solution.py:226
  1215.0 98.7 %reduce-scatter.16.cloned.1.call-done = f32[1536,96]{0,1:T(8,128)} async-done(((f32[1536,768]{0,1:T(8,128)}), f32[1536,96]{0,1:T(8,128)}) %reduce-scatter.16.cloned.1.call-update) | async-done | bytes 589840 | tf_op jit(solution)/shard_map/reduce_scatter | solution.py:228
  1313.7 83.0 %reduce-scatter.10.cloned.1.call-done = f32[96,3,384]{2,0,1:T(8,128)} async-done(((f32[768,3,384]{2,0,1:T(8,128)}), f32[96,3,384]{2,0,1:T(8,128)}) %reduce-scatter.10.cloned.1.call-update) | async-done | bytes 442384 | tf_op jit(solution)/shard_map/reduce_scatter | solution.py:223
  1396.7 7.0 add_add_fusion.2
  1408.6 8.2 copy.190
  1416.8 44.6 %reduce-scatter.18.cloned.1.call-done = f32[96,6]{1,0:T(8,128)} async-done(((f32[768,6]{1,0:T(8,128)}), f32[96,6]{1,0:T(8,128)}) %reduce-scatter.18.cloned.1.call-update) | async-done | bytes 2320
  1468.7 15.1 %all-reduce.19.cloned.1.call-done = (f32[96,3,384]{2,0,1:T(8,128)}, f32[384,96]{0,1:T(8,128)}, f32[96,1536]{1,0:T(8,128)}, f32[1536,96]{0,1:T(8,128)}) async-done(((f32[96,3,384]{2,0,1:T(8,128)}, f32[384,96]{0,1:T(8,128)}, f32[96,1536]{1,0:T(8,128)}, f32[1536,96]{0,1:T(8,128)}), (f32[96,3,384]{2,0,1:T(8,128)}, f32[384,96]{0,1:T(8,128)}, f32[96,1536]{1,0:T(8,128)}, ...) | async-done | bytes 1769488 | tf_op jit(solution)/shard_map/psum | solution.py:239
  (399 shorter events, 434.2 us)
Async XLA Ops:
  7.2 55.7 %all-gather.7.cloned.1.call-start = ((), (), s32[]{:S(2)}) async-start(), calls=%async_computation.5 | async-start | bytes 1990656 | tf_op jit(solution)/shard_map/all_gather | solution.py:67
  9.2 152.2 %all-gather.9.cloned.1.call-start = ((), (), s32[]{:S(2)}) async-start(), calls=%async_computation.6 | async-start | bytes 3456000 | tf_op jit(solution)/shard_map/all_gather | solution.py:97
  53.5 406.5 %copy-start.42 = (f32[768]{0:T(1024)}, f32[768]{0:T(1024)S(1)}, u32[]{:S(2)}) copy-start(f32[768]{0:T(1024)S(1)} %get-tuple-element.457) | copy-start | bytes 9220
  79.5 85.2 %all-gather.11.cloned.1.call-start = ((), (), s32[]{:S(2)}) async-start(), calls=%async_computation.7 | async-start | bytes 3456000 | tf_op jit(solution)/shard_map/all_gather | solution.py:98
  122.4 282.9 %all-reduce.15.cloned.1.call-start = ((), (), s32[]{:S(2)}) async-start(), calls=%async_computation.8 | async-start | bytes 9240576 | tf_op jit(solution)/shard_map/psum | solution.py:128
  288.8 171.2 %all-gather.13.cloned.1.call-start = ((), (), s32[]{:S(2)}) async-start(), calls=%async_computation.9 | async-start | bytes 2654208 | tf_op jit(solution)/shard_map/all_gather | solution.py:69
  290.7 222.6 %all-gather.15.cloned.1.call-start = ((), (), s32[]{:S(2)}) async-start(), calls=%async_computation.10 | async-start | bytes 2654208 | tf_op jit(solution)/shard_map/all_gather | solution.py:70
  292.6 371.3 %all-reduce.17.cloned.1.call-start = ((), (), s32[]{:S(2)}) async-start(), calls=%async_computation.11 | async-start | bytes 9240576 | tf_op jit(solution)/shard_map/psum | solution.py:153
  548.2 501.5 %all-reduce.21.cloned.1.call-start = ((), (), s32[]{:S(2)}) async-start(), calls=%async_computation.18 | async-start | bytes 9240576 | tf_op jit(solution)/shard_map/psum | solution.py:138
  932.0 195.0 %reduce-scatter.12.cloned.1.call-start = ((), (), s32[]{:S(2)}) async-start(), calls=%async_computation.13 | async-start | bytes 1327104 | tf_op jit(solution)/shard_map/reduce_scatter | solution.py:225
  937.4 277.6 %reduce-scatter.14.cloned.1.call-start = ((), (), s32[]{:S(2)}) async-start(), calls=%async_computation.14 | async-start | bytes 5308416 | tf_op jit(solution)/shard_map/reduce_scatter | solution.py:226
  948.2 365.5 %reduce-scatter.16.cloned.1.call-start = ((), (), s32[]{:S(2)}) async-start(), calls=%async_computation.15 | async-start | bytes 5308416 | tf_op jit(solution)/shard_map/reduce_scatter | solution.py:228
  956.1 93.6 %copy-start.25 = (f32[768]{0:T(1024)S(1)}, f32[768]{0:T(1024)}, u32[]{:S(2)}) copy-start(f32[768]{0:T(1024)} %copy-done.24) | copy-start | bytes 9220
  956.2 98.2 %copy-start.31 = (f32[768]{0:T(1024)S(1)}, f32[768]{0:T(1024)}, u32[]{:S(2)}) copy-start(f32[768]{0:T(1024)} %copy-done.30) | copy-start | bytes 9220
  956.2 440.5 %reduce-scatter.10.cloned.1.call-start = ((), (), s32[]{:S(2)}) async-start(), calls=%async_computation.12 | async-start | bytes 3981312 | tf_op jit(solution)/shard_map/reduce_scatter | solution.py:223
  957.3 97.1 %copy-start.10 = (bf16[1500,1,384]{2,0,1:T(8,128)(2,1)S(1)}, bf16[1500,1,384]{2,0,1:T(8,128)(2,1)}, u32[]{:S(2)}) copy-start(bf16[1500,1,384]{2,0,1:T(8,128)(2,1)} %stack.24) | copy-start | bytes 3456004
  1062.3 399.2 %reduce-scatter.18.cloned.1.call-start = ((), (), s32[]{:S(2)}) async-start(), calls=%async_computation.16 | async-start | bytes 442368
  1118.7 365.1 %all-reduce.19.cloned.1.call-start = ((), (), s32[]{:S(2)}) async-start(), calls=%async_computation.17 | async-start | bytes 3538944 | tf_op jit(solution)/shard_map/psum | solution.py:239
  1408.5 57.1 %copy-start.37 = (f32[2,6,8]{2,0,1:T(2,128)S(1)}, f32[2,6,8]{2,0,1:T(2,128)}, u32[]{:S(2)}) copy-start(f32[2,6,8]{2,0,1:T(2,128)} %param.34) | copy-start | bytes 1156
  1408.5 59.0 %copy-start.33 = (f32[24,8]{0,1:T(8,128)S(1)}, f32[24,8]{0,1:T(8,128)}, u32[]{:S(2)}) copy-start(f32[24,8]{0,1:T(8,128)} %param.41) | copy-start | bytes 2308
  1408.5 59.0 %copy-start.38 = (f32[24,8]{0,1:T(8,128)S(1)}, f32[24,8]{0,1:T(8,128)}, u32[]{:S(2)}) copy-start(f32[24,8]{0,1:T(8,128)} %param.42) | copy-start | bytes 2308
  1408.5 58.9 %copy-start.39 = (f32[24,8]{0,1:T(8,128)S(1)}, f32[24,8]{0,1:T(8,128)}, u32[]{:S(2)}) copy-start(f32[24,8]{0,1:T(8,128)} %param.43) | copy-start | bytes 2308
  1408.5 59.6 %copy-start.34 = (f32[6,96]{1,0:T(8,128)S(1)}, f32[6,96]{1,0:T(8,128)}, u32[]{:S(2)}) copy-start(f32[6,96]{1,0:T(8,128)} %param.47) | copy-start | bytes 6916
  1408.6 59.5 %copy-start.40 = (f32[6,96]{1,0:T(8,128)S(1)}, f32[6,96]{1,0:T(8,128)}, u32[]{:S(2)}) copy-start(f32[6,96]{1,0:T(8,128)} %param.48) | copy-start | bytes 6916
  1408.6 59.5 %copy-start.41 = (f32[6,96]{1,0:T(8,128)S(1)}, f32[6,96]{1,0:T(8,128)}, u32[]{:S(2)}) copy-start(f32[6,96]{1,0:T(8,128)} %param.49) | copy-start | bytes 6916
  1408.6 75.3 %copy-start.17 = (f32[96,3,384]{2,0,1:T(8,128)S(1)}, f32[96,3,384]{2,0,1:T(8,128)}, u32[]{:S(2)}) copy-start(f32[96,3,384]{2,0,1:T(8,128)} %param.29) | copy-start | bytes 1327108
  1408.6 75.3 %copy-start.23 = (f32[96,3,384]{2,0,1:T(8,128)S(1)}, f32[96,3,384]{2,0,1:T(8,128)}, u32[]{:S(2)}) copy-start(f32[96,3,384]{2,0,1:T(8,128)} %param.30) | copy-start | bytes 1327108
  1408.6 77.7 %copy-start.19 = (f32[384,96]{0,1:T(8,128)S(1)}, f32[384,96]{0,1:T(8,128)}, u32[]{:S(2)}) copy-start(f32[384,96]{0,1:T(8,128)} %param.35) | copy-start | bytes 442372
  1408.6 79.6 %copy-start.14 = (f32[96,1536]{1,0:T(8,128)S(1)}, f32[96,1536]{1,0:T(8,128)}, u32[]{:S(2)}) copy-start(f32[96,1536]{1,0:T(8,128)} %param.38) | copy-start | bytes 1769476
  1408.6 79.6 %copy-start.20 = (f32[96,1536]{1,0:T(8,128)S(1)}, f32[96,1536]{1,0:T(8,128)}, u32[]{:S(2)}) copy-start(f32[96,1536]{1,0:T(8,128)} %param.39) | copy-start | bytes 1769476
  1408.6 79.6 %copy-start.21 = (f32[96,1536]{1,0:T(8,128)S(1)}, f32[96,1536]{1,0:T(8,128)}, u32[]{:S(2)}) copy-start(f32[96,1536]{1,0:T(8,128)} %param.40) | copy-start | bytes 1769476
  1416.8 74.0 %copy-start.15 = (f32[1536,96]{0,1:T(8,128)S(1)}, f32[1536,96]{0,1:T(8,128)}, u32[]{:S(2)}) copy-start(f32[1536,96]{0,1:T(8,128)} %param.44) | copy-start | bytes 1769476
  (30 other events, 362.2 us)
Sparse Core Ops, SparseCore 0:
  10.8 48.7 all-gather.6
  79.6 10.3 all-gather.8
  122.5 10.3 all-gather.10
  288.9 116.3 all-reduce.14
  407.9 52.0 all-gather.12
  462.6 50.5 all-gather.14
  548.3 115.5 all-reduce.16
  932.1 117.4 all-reduce.20
  1053.1 64.1 reduce-scatter.11
  1120.7 94.1 reduce-scatter.13
  1218.6 94.9 reduce-scatter.15
  1317.7 78.9 reduce-scatter.9
  1400.5 60.8 reduce-scatter.17
  1463.9 19.9 all-reduce.18
where the time goes:
time: 1510 us; the launch traced here: 1500 us
  waiting for transfers between devices  681 us (45%)
  matrix products  293 us (19%)
  blocking collectives  187 us (12%)
  local copies, waits for them, and re-layouts  164 us (11%)
  other arithmetic  111 us (7%)
  loops' own time  47.8 us (3%)
  between operations  16 us (1%)
    reduce_scatter x1, waiting for transfers between devices, local(): lax.psum_scatter(grad_reduce, 'fsdp', scatter_dimension=1, tiled=True)  98.7 us
    psum x1, waiting for transfers between devices, local(): lax.psum(jnp.einsum('nf,df->nd', grad_expanded, expand_full, preferred_el...  94 us
    psum x1, waiting for transfers between devices, local(): lax.psum(jnp.dot(activated, reduce_full, preferred_element_type=single).a...  92.2 us
    reduce_scatter x1, waiting for transfers between devices, local(): lax.psum_scatter(grad_expand, 'fsdp', scatter_dimension=0, tiled=True)  87.9 us
    reduce_scatter x1, waiting for transfers between devices, local(): lax.psum_scatter(grad_attend, 'fsdp', scatter_dimension=0, tiled=True)  83 us
    psum x1, waiting for transfers between devices, local(): lax.psum(jnp.dot(attended, output_full, preferred_element_type=single), '...  74.7 us
    unnamed x2, blocking collectives  64.9 us
    all_gather x1, waiting for transfers between devices, local(): lax.all_gather(expand_weight.astype(bfloat), 'fsdp', axis=0, tiled=True)  47.6 us
  transfers between devices with their start and end apart: 14, of which 10 were waited for; matrix products, arithmetic and copies ran while one was open for 12% of the time, Pallas kernels for 0%

commit v1 on v0

v1 whole, which is shorter than its diff:
```python
import functools
import math

import jax
import jax.numpy as jnp
from jax import lax
from jax.experimental import pallas as pl
from jax.experimental.pallas import tpu as pltpu
from jax.sharding import PartitionSpec as P

HD = 64
STEP = 10


norm_eps = 1e-05
beta_first = 0.9
beta_second = 0.999
adam_eps = 1e-08
rate_matrix = 0.05
rate_vector = 0.5
decay_matrix = 0.01

bfloat = jnp.bfloat16
single = jnp.float32
LANES = 128
QUERY_ROWS = 256
KEY_ROWS = 256
TOKEN_ROWS = 256
SWAP = [(0, 1), (1, 0)]
EXP_SCALE = HD ** (-0.5) * math.log2(math.e)
MASK = -1e30
VMEM = 56 * 1024 * 1024
NT = (((1,), (1,)), ((), ()))
TN = (((0,), (0,)), ((), ()))


def dot(left, right, dims=(((1,), (0,)), ((), ()))):
    return lax.dot_general(left, right, dims, preferred_element_type=single)


def adamw(param, grad, moment, square, rate, decay):
    moment_new = beta_first * moment + (1.0 - beta_first) * grad
    square_new = beta_second * square + (1.0 - beta_second) * grad * grad
    corrected = moment_new / (1.0 - beta_first**STEP)
    normal_sq = square_new / (1.0 - beta_second**STEP)
    param_new = param - rate * (corrected / (jnp.sqrt(normal_sq) + adam_eps) + decay * param)
    return (param_new, moment_new, square_new)


def norm_parts(values):
    average = jnp.mean(values, axis=-1, keepdims=True)
    centered = values - average
    variance = jnp.mean(centered * centered, axis=-1, keepdims=True)
    inverse = lax.rsqrt(variance + norm_eps)
    return centered * inverse, inverse


def norm_back(grad, unit, inverse, gain):
    scaled = grad * gain
    first = jnp.mean(scaled, axis=-1, keepdims=True)
    second = jnp.mean(scaled * unit, axis=-1, keepdims=True)
    return (scaled - first - unit * second) * inverse


def split_three(column):
    high = column.astype(bfloat).astype(single)
    rest = column - high
    middle = rest.astype(bfloat).astype(single)
    return high, middle, (rest - middle).astype(bfloat).astype(single)


def beside(values, half, extras):
    lane = lax.broadcasted_iota(jnp.int32, values.shape, 1)
    base = HD * (1 - half)
    mine = (lane >= HD) if half else (lane < HD)
    out = jnp.where(mine, values, 0.0)
    for place, extra in enumerate(extras):
        out = jnp.where(lane == base + place, extra, out)
    return out.astype(bfloat)


def pad_column(first_row, rows, period, valid):
    row = first_row + lax.broadcasted_iota(jnp.int32, (rows, 1), 0)
    return jnp.where(row % period < valid, 0.0, MASK)


def attend_kernel(period, valid, q_ref, k_ref, v_ref, o_ref, lse_ref, keys, values):
    @pl.when(pl.program_id(1) == 0)
    def _():
        k = k_ref[...].astype(single)
        v = v_ref[...].astype(single)
        pad = pad_column(0, k.shape[0], period, valid)
        for half in range(2):
            keys[half] = beside(k, half, (pad,))
            values[half] = beside(v, half, (1.0,))

    q = q_ref[...].astype(single)
    lane = lax.broadcasted_iota(jnp.int32, q.shape, 1)
    outs, tops = [], []
    for half in range(2):
        scores = dot(beside(q, half, (1.0,)), keys[half], NT)
        top = jnp.max(scores, axis=1, keepdims=True)
        raised = jnp.exp2((scores - top) * EXP_SCALE)
        both = dot(raised.astype(bfloat), values[half])
        base = HD * (1 - half)
        total = jnp.sum(jnp.where(lane == base, both, 0.0), axis=1, keepdims=True)
        outs.append(both / total)
        tops.append(top + jnp.log2(total) / EXP_SCALE)
    o_ref[...] = jnp.where(lane < HD, outs[0], outs[1]).astype(bfloat)
    lse_ref[...] = jnp.where(lane < HD, tops[0], tops[1])


def attend(qkv, period, valid):
    rows, width = qkv.shape[0], qkv.shape[1] // 3
    pairs = width // LANES
    whole = lambda part: pl.BlockSpec((rows, LANES), lambda j, i: (0, part * pairs + j))
    block = pl.BlockSpec((QUERY_ROWS, LANES), lambda j, i: (i, j))
    return pl.pallas_call(
        functools.partial(attend_kernel, period, valid),
        grid=(pairs, rows // QUERY_ROWS),
        in_specs=[block, whole(1), whole(2)],
        out_specs=[block, block],
        out_shape=[
            jax.ShapeDtypeStruct((rows, width), bfloat),
            jax.ShapeDtypeStruct((rows, width), single),
        ],
        scratch_shapes=[
            pltpu.VMEM((2, rows, LANES), bfloat),
            pltpu.VMEM((2, rows, LANES), bfloat),
        ],
        compiler_params=pltpu.CompilerParams(vmem_limit_bytes=VMEM),
        cost_estimate=pl.CostEstimate(
            flops=16 * rows * rows * LANES * pairs,
            bytes_accessed=20 * rows * width,
            transcendentals=2 * pairs * rows * rows,
        ),
        name="attend",
    )(qkv, qkv, qkv)


def attend_back_kernel(
    period, valid, q_ref, k_ref, v_ref, o_ref, lse_ref, g_ref,
    dq_ref, dk_ref, dv_ref, queries, grads, total,
):
    step = pl.program_id(1)
    lane_all = lax.broadcasted_iota(jnp.int32, q_ref.shape, 1)

    @pl.when(step == 0)
    def _():
        q = q_ref[...].astype(single)
        g = g_ref[...].astype(single)
        product = g * o_ref[...].astype(single)
        for half in range(2):
            mine = (lane_all >= HD) if half else (lane_all < HD)
            inner = jnp.sum(jnp.where(mine, product, 0.0), axis=1, keepdims=True)
            low = jnp.max(jnp.where(mine, lse_ref[...], -jnp.inf), axis=1, keepdims=True)
            queries[half] = beside(q, half, (1.0,) + split_three(-low))
            grads[half] = beside(g, half, (0.0,) + split_three(-inner))
        total[...] = jnp.zeros_like(total)

    k = k_ref[...].astype(single)
    v = v_ref[...].astype(single)
    pad = pad_column(step * k.shape[0], k.shape[0], period, valid)
    lane = lax.broadcasted_iota(jnp.int32, k.shape, 1)
    dks, dvs, dqs = [], [], []
    for half in range(2):
        keys = beside(k, half, (pad, 1.0, 1.0, 1.0))
        values = beside(v, half, (1.0, 1.0, 1.0, 1.0))
        weights = jnp.exp2(dot(keys, queries[half], NT) * EXP_SCALE)
        inner = weights * dot(values, grads[half], NT)
        dvs.append(dot(weights.astype(bfloat), grads[half]))
        low = inner.astype(bfloat)
        dks.append(dot(low, queries[half]))
        dqs.append(dot(keys, low, TN))
    scale = HD ** (-0.5)
    dk_ref[...] = (jnp.where(lane < HD, dks[0], dks[1]) * scale).astype(bfloat)
    dv_ref[...] = jnp.where(lane < HD, dvs[0], dvs[1]).astype(bfloat)
    row = lax.broadcasted_iota(jnp.int32, total.shape, 0)
    total[...] += jnp.where(row < HD, dqs[0], dqs[1])

    @pl.when(step == pl.num_programs(1) - 1)
    def _():
        dq_ref[...] = (total[...].T * scale).astype(bfloat)


def attend_back(qkv, o, lse, grad, period, valid):
    rows, width = o.shape
    pairs = width // LANES
    whole = pl.BlockSpec((rows, LANES), lambda j, i: (0, j))
    part = lambda at: pl.BlockSpec((KEY_ROWS, LANES), lambda j, i: (i, at * pairs + j))
    block = pl.BlockSpec((KEY_ROWS, LANES), lambda j, i: (i, j))
    return pl.pallas_call(
        functools.partial(attend_back_kernel, period, valid),
        grid=(pairs, rows // KEY_ROWS),
        in_specs=[whole, part(1), part(2), whole, whole, whole],
        out_specs=[whole, block, block],
        out_shape=[jax.ShapeDtypeStruct((rows, width), bfloat)] * 3,
        scratch_shapes=[
            pltpu.VMEM((2, rows, LANES), bfloat),
            pltpu.VMEM((2, rows, LANES), bfloat),
            pltpu.VMEM((LANES, rows), single),
        ],
        compiler_params=pltpu.CompilerParams(vmem_limit_bytes=VMEM),
        cost_estimate=pl.CostEstimate(
            flops=40 * rows * rows * LANES * pairs,
            bytes_accessed=20 * rows * width,
            transcendentals=2 * pairs * rows * rows,
        ),
        name="attend_back",
    )(qkv, qkv, qkv, o, lse, grad)


def forward_kernel(n_ref, g_ref, w1_ref, w2_ref, b_ref, y_ref, dn_ref, act_ref, du_ref):
    normed = n_ref[...]
    grad = g_ref[...]
    count, _, units = w1_ref.shape
    mixed = back = 0.0
    for part in range(count):
        cols = slice(part * units, (part + 1) * units)
        u = dot(normed, w1_ref[part]) + b_ref[:, cols]
        phi = 0.5 * (1.0 + lax.erf(u * (0.5**0.5)))
        act = (u * phi).astype(bfloat)
        slope = phi + u * (jnp.exp(-0.5 * u * u) * ((2.0 * math.pi) ** -0.5))
        du = (dot(grad, w2_ref[part]) * slope).astype(bfloat)
        act_ref[:, cols] = act
        du_ref[:, cols] = du
        mixed = mixed + dot(act, w2_ref[part], NT)
        back = back + dot(du, w1_ref[part], NT)
    y_ref[...] = mixed.astype(bfloat)
    dn_ref[...] = back.astype(bfloat)


def feed_forward(normed, grad, weights, bias):
    rows, width = normed.shape
    count = weights.shape[0]
    hidden = bias.shape[1]
    units = hidden // count
    tokens = pl.BlockSpec((TOKEN_ROWS, width), lambda i: (i, 0))
    wide = pl.BlockSpec((TOKEN_ROWS, hidden), lambda i: (i, 0))
    weight = lambda at: pl.BlockSpec((count, width, units), lambda i: (0, 0, at))
    return pl.pallas_call(
        forward_kernel,
        grid=(rows // TOKEN_ROWS,),
        in_specs=[tokens, tokens, weight(0), weight(1), pl.BlockSpec((1, hidden), lambda i: (0, 0))],
        out_specs=[tokens, tokens, wide, wide],
        out_shape=[
            jax.ShapeDtypeStruct((rows, width), bfloat),
            jax.ShapeDtypeStruct((rows, width), bfloat),
            jax.ShapeDtypeStruct((rows, hidden), bfloat),
            jax.ShapeDtypeStruct((rows, hidden), bfloat),
        ],
        compiler_params=pltpu.CompilerParams(vmem_limit_bytes=VMEM),
        cost_estimate=pl.CostEstimate(
            flops=8 * rows * width * hidden,
            bytes_accessed=8 * rows * width + 4 * rows * hidden + 4 * width * hidden,
            transcendentals=2 * rows * hidden,
        ),
        name="feed_forward",
    )(normed, grad, weights, weights, bias)


def swap_core(value):
    return lax.ppermute(value, "ctx", SWAP)


def join(mine, other, first, axis):
    return jnp.concatenate([jnp.where(first, mine, other), jnp.where(first, other, mine)], axis=axis)


def take(value, index, axis=0):
    return lax.dynamic_index_in_dim(value, index, axis, keepdims=False)


def sum_over_tp(value):
    at = lax.axis_index("tp")
    away = lax.ppermute(take(value, 1 - at).astype(bfloat), "tp", SWAP)
    return take(value, at) + away.astype(single)


def sum_over_near(value, axis):
    at = lax.axis_index("fsdp") % 2
    pairs = [(i, i ^ 1) for i in range(lax.axis_size("fsdp"))]
    away = lax.ppermute(take(value, 1 - at, axis).astype(bfloat), "fsdp", pairs)
    return take(value, at, axis) + away.astype(single)


def sum_over_far(value):
    size = lax.axis_size("fsdp")
    far = size // 2
    at = lax.axis_index("fsdp") // 2
    low = value.astype(bfloat)
    total = take(value, at)
    for step in range(1, far):
        pairs = [(i, (i + 2 * step) % size) for i in range(size)]
        total = total + lax.ppermute(take(low, (at + step) % far), "fsdp", pairs).astype(single)
    return total


def scatter(value, near_first):
    size = lax.axis_size("fsdp")
    count, width, columns = value.shape
    rows = width // size
    if near_first:
        value = sum_over_near(value.reshape(count, size // 2, 2, rows, columns), 2)
        value = sum_over_tp(value)
    else:
        value = sum_over_tp(value.reshape(count, size // 2, 2, rows, columns))
        value = sum_over_near(value, 1)
    return sum_over_far(value)


def local(
    layer_input,
    cotangent,
    attend_weight,
    attend_moment,
    attend_square,
    shifts_weight,
    shifts_moment,
    shifts_square,
    output_weight,
    output_moment,
    output_square,
    expand_weight,
    expand_moment,
    expand_square,
    offset_weight,
    offset_moment,
    offset_square,
    reduce_weight,
    reduce_moment,
    reduce_square,
    vectors_weight,
    vectors_moment,
    vectors_square,
):
    size = lax.axis_size("fsdp")
    tps = lax.axis_size("tp")
    core, half = lax.axis_index("ctx"), lax.axis_index("tp")
    first_core, first_tp = core == 0, half == 0
    _, frames, width = layer_input.shape
    period = -(-frames // TOKEN_ROWS) * TOKEN_ROWS
    pad = lambda a: jnp.pad(a, ((0, period - frames), (0, 0)))
    shard = attend_weight.shape[0]
    cols = attend_weight.shape[2] // 2
    heads = cols // HD
    units = expand_weight.shape[1] // 2
    hidden = tps * units

    low = lambda a: a.astype(bfloat)
    attend_mine = lax.dynamic_slice_in_dim(low(attend_weight), core * cols, cols, 2)
    small_mine = jnp.concatenate(
        [low(shifts_weight).reshape(-1), low(offset_weight).reshape(-1), low(vectors_weight).reshape(-1)]
    )
    small_cols = small_mine.size // shard
    pack_one = jnp.concatenate(
        [
            attend_mine.reshape(shard, 3 * cols),
            small_mine.reshape(shard, small_cols),
            jnp.zeros((shard, HD - small_cols), bfloat),
        ],
        axis=1,
    )
    all_one = lax.all_gather(pack_one, ("tp", "fsdp"), axis=0, tiled=True)
    expand_mine = lax.dynamic_slice_in_dim(low(expand_weight), core * units, units, 1)
    reduce_mine = lax.dynamic_slice_in_dim(low(reduce_weight), core * units, units, 0).T
    output_mine = lax.dynamic_slice_in_dim(low(output_weight), core * cols, cols, 0).T
    pack_two = jnp.concatenate(
        [expand_mine, reduce_mine, output_mine, jnp.zeros((shard, HD), bfloat)], axis=1
    )
    pack_two, all_one = lax.optimization_barrier((pack_two, all_one))
    all_two = lax.all_gather(pack_two, ("tp", "fsdp"), axis=0, tiled=True)

    x_mine = pad(take(layer_input, half))
    g_mine = pad(take(cotangent, half))
    tokens = jnp.concatenate([x_mine, swap_core(x_mine)]).astype(single)
    grad_mixed = jnp.concatenate([g_mine, swap_core(g_mine)])

    all_one = all_one.reshape(tps, width, 3 * cols + HD)
    w_attend = all_one[:, :, : 3 * cols].reshape(tps, width, 3, cols)
    w_attend = w_attend.transpose(1, 2, 0, 3).reshape(width, 3 * tps * cols)
    small = all_one[:, :, 3 * cols : 3 * cols + small_cols].reshape(tps, size, -1)
    n_shift, n_offset = shifts_weight.size, offset_weight.size
    shifts = small[:, :, :n_shift].reshape((tps, size) + shifts_weight.shape)
    shifts = shifts.transpose(2, 0, 3, 1, 4).reshape(2, tps, 2 * heads, HD)
    shifts = lax.dynamic_slice_in_dim(shifts, core * heads, heads, 2).reshape(2, 1, tps * cols)
    offset = small[:, :, n_shift : n_shift + n_offset].reshape((tps, size) + offset_weight.shape)
    offset = offset.transpose(0, 2, 1, 3).reshape(tps, 2, units)
    offset = take(offset, core, 1).reshape(1, hidden).astype(single)
    vectors = small[0, :, n_shift + n_offset :].reshape((size,) + vectors_weight.shape)
    vectors = vectors.transpose(1, 0, 2).reshape(-1, 1, width).astype(single)
    bias = jnp.concatenate([shifts[0], jnp.zeros_like(shifts[0]), shifts[1]], axis=1).astype(single)

    unit_one, inverse_one = norm_parts(tokens)
    normed_one = low(unit_one * vectors[0] + vectors[1])
    qkv = low(dot(normed_one, w_attend) + bias)
    attended, lse = attend(qkv, period, frames)

    all_two = all_two.reshape(tps, width, -1)
    w_output = all_two[:, :, 2 * units : 2 * units + cols].transpose(1, 0, 2)
    w_output = w_output.reshape(width, tps * cols)
    branch = low(dot(attended, w_output, NT))
    other = swap_core(branch)

    def with_other(mine, other):
        turned = jnp.concatenate([other[period:], other[:period]])
        return mine.astype(single) + turned.astype(single)

    hidden_one = tokens + with_other(branch, other) + vectors[2]
    unit_two, inverse_two = norm_parts(hidden_one)
    normed_two = low(unit_two * vectors[3] + vectors[4])
    mixed, back, act, du = feed_forward(normed_two, grad_mixed, all_two, offset)
    back_other = swap_core(back)
    mixed_other = swap_core(mixed[period:])
    block = hidden_one[:period] + mixed[:period].astype(single) + mixed_other.astype(single)
    block = low(block + vectors[5])[:frames]
    block_output = join(block[None], lax.ppermute(block, "tp", SWAP)[None], first_tp, 0)

    grad_expand = jnp.stack([dot(normed_two, du[:, t * units : (t + 1) * units], TN) for t in range(tps)])
    grad_reduce = jnp.stack([dot(grad_mixed, act[:, t * units : (t + 1) * units], TN) for t in range(tps)])
    grad_offset = jnp.sum(du.astype(single), axis=0)

    grad_normed = with_other(back, back_other)
    grad_hidden = grad_mixed.astype(single) + norm_back(grad_normed, unit_two, inverse_two, vectors[3])
    grad_branch = low(grad_hidden)
    grad_attended = low(dot(grad_branch, w_output))
    dq, dk, dv = attend_back(qkv, attended, lse, grad_attended, period, frames)
    grad_output = dot(grad_branch, attended, TN).reshape(width, tps, cols).transpose(1, 0, 2)
    grad_qkv = jnp.concatenate([dq, dk, dv], axis=1)
    grad_attend = dot(normed_one, grad_qkv, TN).reshape(width, 3, tps, cols)
    grad_attend = grad_attend.transpose(2, 0, 1, 3).reshape(tps, width, 3 * cols)
    back_one = low(dot(grad_qkv, w_attend, NT))
    back_one = back_one[:period].astype(single) + swap_core(back_one[period:]).astype(single)
    unit_own = unit_one[:period]
    grad_tokens = norm_back(back_one, unit_own, inverse_one[:period], vectors[0])
    input_own = low(grad_hidden[:period] + grad_tokens)[:frames]
    input_grad = join(input_own[None], lax.ppermute(input_own, "tp", SWAP)[None], first_tp, 0)
    input_grad = input_grad.astype(single)

    total = lambda a: jnp.sum(a, axis=0)
    own = grad_normed[:period]
    grad_vectors = jnp.stack(
        [
            total(back_one * unit_own),
            total(back_one),
            total(grad_branch[:period].astype(single)),
            total(own * unit_two[:period]),
            total(own),
            total(g_mine.astype(single)),
        ]
    )
    grad_shifts = jnp.stack([total(dq.astype(single)), total(dv.astype(single))])
    grad_shifts = grad_shifts.reshape(2, tps, 1, cols)
    grad_shifts = jnp.where(jnp.arange(2).reshape(1, 1, 2, 1) == core, grad_shifts, 0.0)
    grad_offset = grad_offset.reshape(tps, 1, units)
    grad_offset = jnp.where(jnp.arange(2).reshape(1, 2, 1) == core, grad_offset, 0.0)
    flat = jnp.concatenate([grad_vectors.reshape(-1), grad_shifts.reshape(-1), grad_offset.reshape(-1)])
    flat = lax.psum(flat.reshape(-1, LANES), ("fsdp", "ctx", "tp")).reshape(-1)
    n_vectors, n_shifts = grad_vectors.size, grad_shifts.size
    at = lax.axis_index("fsdp")
    total_vectors = take(flat[:n_vectors].reshape(6, size, -1), at, 1)
    total_shifts = take(flat[n_vectors : n_vectors + n_shifts].reshape(2, tps, 2 * heads, HD), half, 1)
    total_shifts = take(total_shifts.reshape(2, 2 * heads, size, -1), at, 2)
    total_offset = take(flat[n_vectors + n_shifts :].reshape((tps,) + offset_weight.shape[:1] + (size, -1)), half)
    total_offset = take(total_offset, at, 1)

    sums = [
        scatter(grad_expand, False),
        scatter(grad_reduce, True),
        scatter(jnp.concatenate([grad_attend, grad_output], axis=2), False),
    ]
    mine = jnp.concatenate(sums, axis=1)
    other = swap_core(mine)

    def both(lo, hi, shape=()):
        a, b = mine[:, lo:hi], other[:, lo:hi]
        if shape:
            a, b = a.reshape(shape), b.reshape(shape)
        return join(a, b, first_core, a.ndim - 1)

    total_expand = both(0, units)
    total_reduce = both(units, 2 * units).T
    total_attend = both(2 * units, 2 * units + 3 * cols, (shard, 3, cols))
    total_output = both(2 * units + 3 * cols, 2 * units + 4 * cols).T

    attend_new = adamw(
        attend_weight, total_attend, attend_moment, attend_square, rate_matrix, decay_matrix
    )
    shifts_new = adamw(shifts_weight, total_shifts, shifts_moment, shifts_square, rate_vector, 0.0)
    output_new = adamw(
        output_weight, total_output, output_moment, output_square, rate_matrix, decay_matrix
    )
    expand_new = adamw(
        expand_weight, total_expand, expand_moment, expand_square, rate_matrix, decay_matrix
    )
    offset_new = adamw(offset_weight, total_offset, offset_moment, offset_square, rate_vector, 0.0)
    reduce_new = adamw(
        reduce_weight, total_reduce, reduce_moment, reduce_square, rate_matrix, decay_matrix
    )
    vectors_new = adamw(
        vectors_weight, total_vectors, vectors_moment, vectors_square, rate_vector, 0.0
    )
    return (
        block_output,
        input_grad,
        *attend_new,
        *shifts_new,
        *output_new,
        *expand_new,
        *offset_new,
        *reduce_new,
        *vectors_new,
    )


def solution(mesh):
    tokens = (P("fsdp", "ctx", None),) * 2
    params = (
        (P("fsdp", None, "tp"),) * 3
        + (P(None, "tp", "fsdp"),) * 3
        + (P("tp", "fsdp"),) * 3
        + (P("fsdp", "tp"),) * 3
        + (P("tp", "fsdp"),) * 3
        + (P("tp", "fsdp"),) * 3
        + (P(None, "fsdp"),) * 3
    )
    return jax.shard_map(
        local,
        mesh=mesh,
        in_specs=tokens + params,
        out_specs=tokens + params,
        check_vma=False,
    )
```

time: 1510 us -> 579 us (0.38)
  waiting for transfers between devices: 681 us -> 151 us
  matrix products: 293 us -> 38.1 us
  blocking collectives: 187 us -> 49.5 us
  Pallas kernels: 0 us -> 97.8 us
  loops' own time: 47.8 us -> 0 us
  other arithmetic: 111 us -> 68.3 us
  local copies, waits for them, and re-layouts: 164 us -> 124 us
  starting transfers between devices: 1.39 us -> 25.7 us
    psum x4 -> x0, waiting for transfers between devices: 276 us -> none  [the longest x1 94 us: local(): lax.psum(jnp.einsum('nf,df->nd', grad_expanded, expand_full, preferred_el...]
    reduce_scatter x4 -> x0, waiting for transfers between devices: 270 us -> none  [the longest x1 98.7 us: local(): lax.psum_scatter(grad_reduce, 'fsdp', scatter_dimension=1, tiled=True)]
    dot_general x96 -> x10, matrix products: 293 us -> 38.1 us  [dot(): return lax.dot_general(left, right, dims, preferred_element_type=single)]
    all_gather x4 -> x0, blocking collectives: 118 us -> none  [the longest x1 33.6 us: local(): lax.all_gather(output_weight.astype(bfloat), 'fsdp', axis=1, tiled=True)]
    pallas_call x0 -> x3, Pallas kernels: none -> 97.8 us  [the longest x1 46.3 us: attend_back(): pl.pallas_call(functools.partial(attend_back_kernel, period, valid), grid...]
    unnamed x2 -> x0, blocking collectives: 64.9 us -> none
    ppermute x0 -> x24, waiting for transfers between devices: none -> 62.3 us  [the longest x9 28.3 us: sum_over_far(): lax.ppermute(take(low, (at + step) % far), 'fsdp', pairs).astype(single)]
    another operation x2 -> x0, loops' own time: 47.8 us -> none  [the longest x1 24 us: local(): lax.map(attend_grad, (pair_ids, row_tops, row_sums))]
  transfers between devices with their start and end apart: 14 -> 26, of which waited for: 10 -> 13; matrix products, arithmetic and copies ran while one was open for 12% -> 25% of each run, Pallas kernels for 0% -> 5%
where the time goes in v1:
time: 579 us; the launch traced here: 570 us
  waiting for transfers between devices  151 us (26%)
  local copies, waits for them, and re-layouts  124 us (21%)
  Pallas kernels  97.8 us (17%)
  other arithmetic  68.3 us (12%)
  blocking collectives  49.5 us (9%)
  matrix products  38.1 us (7%)
  starting transfers between devices  25.7 us (4%)
  between operations  15.3 us (3%)
    all_gather x1, waiting for transfers between devices, local(): all_one = lax.all_gather(pack_one, ('tp', 'fsdp'), axis=0, tiled=True)  59.1 us
    psum x1, blocking collectives, local(): flat = lax.psum(flat.reshape(-1, LANES), ('fsdp', 'ctx', 'tp')).reshape(-1)  49.5 us
    pallas_call x1, Pallas kernels, attend_back(): pl.pallas_call(functools.partial(attend_back_kernel, period, valid), grid...  46.3 us
    dot_general x10, matrix products, dot(): return lax.dot_general(left, right, dims, preferred_element_type=single)  38.1 us
    pallas_call x1, Pallas kernels, attend(): pl.pallas_call(functools.partial(attend_kernel, period, valid), grid=(pai...  30.9 us
    all_gather x1, waiting for transfers between devices, local(): all_two = lax.all_gather(pack_two, ('tp', 'fsdp'), axis=0, tiled=True)  29.5 us
    unnamed x143, local copies, waits for them, and re-layouts  29.3 us
    ppermute x9, waiting for transfers between devices, sum_over_far(): lax.ppermute(take(low, (at + step) % far), 'fsdp', pairs).astype(single)  28.3 us
  transfers between devices with their start and end apart: 26, of which 13 were waited for; matrix products, arithmetic and copies ran while one was open for 25% of the time, Pallas kernels for 5%

profile of v1, /device:TPU:0, one launch (start us, length us, event | category | flops | bytes accessed | tf_op | source)
XLA Modules:
  0.0 570.1 jit_solution(11004420487618014992)
XLA Ops:
  16.5 59.1 %all-gather.3.cloned.1.call-done = bf16[1536,640]{1,0:T(8,128)(2,1)} async-done(((bf16[96,640]{1,0:T(8,128)(2,1)}), bf16[1536,640]{1,0:T(8,128)(2,1)}) %all-gather.3.cloned.1.call-update) | async-done | bytes 1966096 | tf_op jit(solution)/shard_map/all_gather | solution.py:364
  75.6 7.8 %constant_dynamic-slice_fusion.7 = (bf16[1,750,768]{2,0,1:T(2,128)(2,1)}, bf16[1,750,768]{2,0,1:T(2,128)(2,1)S(1)}) fusion(bf16[2,750,768]{2,0,1:T(2,128)(2,1)S(1)} %copy-done.26, s32[]{:T(128)S(6)} %select_n.220, bf16[2,750,768]{2,0,1:T(2,128)(2,1)} %param.23), kind=kLoop, calls=%fused_computation.163 | loop fusion | bytes 4608004 | tf_op jit(solution)/shard_map/jit(dynamic_index_in_dim)/dynamic_slice | solution.py:271
  90.8 4.1 copy.236
  97.8 6.8 %fusion.q_ref.k_ref.v_ref = bf16[1536,1152]{1,0:T(8,128)(2,1)} fusion(bf16[768,1152]{0,1:T(8,128)(2,1)S(1)} %bitcast.195, f32[1152]{0:T(1024)S(1)} %maximum_convert_fusion.1, f32[768]{0:T(1024)S(1)} %add.372, f32[768]{0:T(1024)S(1)} %mul.387, f32[1536]{0:T(1024)S(1)} %add_rsqrt_fusion.1, f32[1536]{0:T(1024)S(1)} %broadcast_multiply_fusion.3, ...), kind=kOutput, calls=%fused_computation.2 | convolution fusion | flops 2732064768 | bytes 7690752 | tf_op jit(solution)/shard_map/dot_general | solution.py:38
  104.6 30.9 %attend.1 = (bf16[1536,384]{1,0:T(8,128)(2,1)}, f32[1536,384]{1,0:T(8,128)}) custom-call(bf16[1536,1152]{1,0:T(8,128)(2,1)} %fusion.q_ref.k_ref.v_ref, bf16[1536,1152]{1,0:T(8,128)(2,1)} %fusion.q_ref.k_ref.v_ref, bf16[1536,1152]{1,0:T(8,128)(2,1)} %fusion.q_ref.k_ref.v_ref), custom_call_target="tpu_custom_call" | custom-call | flops 14495514624 | bytes 11796480 | tf_op jit(solution)/shard_map/attend/pallas_call | solution.py:118
  135.6 29.5 %all-gather.5.cloned.1.call-done = bf16[1536,1792]{1,0:T(8,128)(2,1)} async-done(((bf16[96,1792]{1,0:T(8,128)(2,1)}), bf16[1536,1792]{1,0:T(8,128)(2,1)}) %all-gather.5.cloned.1.call-update) | async-done | bytes 5505040 | tf_op jit(solution)/shard_map/all_gather | solution.py:372
  167.3 4.4 convolution_convert_fusion.1
  195.4 6.9 %fusion.72 = (f32[1536]{0:T(1024)S(1)}, f32[1536,768]{1,0:T(8,128)S(1)}, f32[1536,768]{1,0:T(8,128)}) fusion(f32[768]{0:T(1024)S(1)} %copy-done.51, bf16[768,768]{1,0:T(8,128)(2,1)S(1)} %get-tuple-element.262, bf16[768,768]{1,0:T(8,128)(2,1)S(1)} %get-tuple-element.261, bf16[1536,768]{1,0:T(8,128)(2,1)} %convolution_convert_fusion.1, ...), kind=kLoop, calls=%fused_computation.204 | loop fusion | flops 17693184 | bytes 16536576 | tf_op jit(solution)/shard_map/reduce_sum | solution.py:51
  206.5 20.6 %feed_forward.1 = (bf16[1536,768]{1,0:T(8,128)(2,1)}, bf16[1536,768]{1,0:T(8,128)(2,1)}, bf16[1536,1536]{1,0:T(8,128)(2,1)}, bf16[1536,1536]{1,0:T(8,128)(2,1)}) custom-call(bf16[1536,768]{1,0:T(8,128)(2,1)} %get-tuple-element.250.n_ref, bf16[1536,768]{1,0:T(8,128)(2,1)} %pad_maximum_fusion.1.g_ref, bf16[2,768,1792]{2,1,0:T(8,128)(2,1)} %bitcast.206, ...), custom_call_target="tpu_custom_call" | custom-call | flops 14495514624 | bytes 23592960 | tf_op jit(solution)/shard_map/feed_forward/pallas_call | solution.py:241
  227.1 4.2 fusion.16
  231.4 4.2 fusion.18
  255.0 10.7 %collective-permute-done.18 = bf16[2,4,96,768]{3,2,1,0:T(8,128)(2,1)} collective-permute-done((bf16[2,4,96,768]{3,2,1,0:T(8,128)(2,1)}, bf16[2,4,96,768]{3,2,1,0:T(8,128)(2,1)}, u32[]{:S(2)}, u32[]{:S(2)}) %collective-permute-start.18) | collective-permute-done | bytes 1179680 | tf_op jit(solution)/shard_map/ppermute | solution.py:283
  269.8 4.2 collective-permute-done.13
  279.9 6.7 %collective-permute-done.19 = bf16[4,96,768]{2,1,0:T(8,128)(2,1)S(1)} collective-permute-done((bf16[4,96,768]{2,1,0:T(8,128)(2,1)S(1)}, bf16[4,96,768]{2,1,0:T(8,128)(2,1)S(1)}, u32[]{:S(2)}, u32[]{:S(2)}) %collective-permute-start.19) | collective-permute-done | bytes 589856 | tf_op jit(solution)/shard_map/ppermute | solution.py:276
  291.2 4.3 collective-permute-done.20
  299.8 8.5 %collective-permute-done.21 = bf16[96,768]{1,0:T(8,128)(2,1)S(1)} collective-permute-done((bf16[96,768]{1,0:T(8,128)(2,1)S(1)}, bf16[96,768]{1,0:T(8,128)(2,1)S(1)}, u32[]{:S(2)}, u32[]{:S(2)}) %collective-permute-start.21) | collective-permute-done | bytes 147488 | tf_op jit(solution)/shard_map/ppermute | solution.py:295
  309.0 6.0 %collective-permute-done.16 = bf16[96,768]{1,0:T(8,128)(2,1)S(1)} collective-permute-done((bf16[96,768]{1,0:T(8,128)(2,1)S(1)}, bf16[96,768]{1,0:T(8,128)(2,1)S(1)}, u32[]{:S(2)}, u32[]{:S(2)}) %collective-permute-start.16) | collective-permute-done | bytes 147488 | tf_op jit(solution)/shard_map/ppermute | solution.py:295
  323.9 5.2 fusion.71
  331.8 46.3 %attend_back.1 = (bf16[1536,384]{1,0:T(8,128)(2,1)}, bf16[1536,384]{1,0:T(8,128)(2,1)}, bf16[1536,384]{1,0:T(8,128)(2,1)}) custom-call(bf16[1536,1152]{1,0:T(8,128)(2,1)} %fusion.q_ref.k_ref.v_ref, bf16[1536,1152]{1,0:T(8,128)(2,1)} %fusion.q_ref.k_ref.v_ref, bf16[1536,1152]{1,0:T(8,128)(2,1)} %fusion.q_ref.k_ref.v_ref, ...), custom_call_target="tpu_custom_call" | custom-call | flops 36238786560 | bytes 11796480 | tf_op jit(solution)/shard_map/attend_back/pallas_call | solution.py:192
  396.4 5.4 convolution_convert_fusion
  404.4 5.3 fusion.35
  410.9 3.5 concatenate.85
  416.7 8.7 %concatenate.84 = f32[2,4,2,96,576]{3,2,1,4,0:T(2,128)} reshape(f32[2,768,3,192]{1,3,2,0:T(8,128)S(1)} %copy.245) | data formatting | bytes 7077888 | tf_op jit(solution)/shard_map/concatenate | solution.py:470
  425.4 4.1 constant_dynamic-update-slice_fusion.4
  433.8 3.6 copy.246
  444.5 6.0 %multiply_reduce_fusion.3 = (f32[768]{0:T(1024)S(1)}, f32[768]{0:T(1024)}, f32[768]{0:T(1024)S(1)}, f32[768]{0:T(1024)}, f32[768,768]{1,0:T(8,128)}, /*index=5*/f32[768,768]{1,0:T(8,128)}) fusion(bf16[768,768]{1,0:T(8,128)(2,1)} %collective-permute-done.6, bf16[1536,768]{1,0:T(8,128)(2,1)} %copy-done.25, f32[1536,768]{1,0:T(8,128)} %get-tuple-element.256, ...), kind=kLoop, calls=%fused_computation.49 | loop fusion | flops 5895168 | bytes 9452544 | tf_op jit(solution)/shard_map/reduce_sum | solution.py:440
  455.3 49.5 %psum.7 = f32[72,128]{1,0:T(8,128)} all-reduce(f32[72,128]{1,0:T(8,128)} %maximum_bitcast_fusion.2), channel_id=1, replica_groups=mesh['fsdp'=8,'ctx'=2,'tp'=2] {'fsdp','ctx','tp'}, use_global_device_ids=true, to_apply=%region_17.18 | all-reduce | flops 9216 | bytes 73728 | tf_op jit(solution)/shard_map/psum | solution.py:458
  524.1 7.6 %collective-permute-done.9 = bf16[4,96,768]{2,1,0:T(8,128)(2,1)S(1)} collective-permute-done((bf16[4,96,768]{2,1,0:T(8,128)(2,1)S(1)}, bf16[4,96,768]{2,1,0:T(8,128)(2,1)S(1)}, u32[]{:S(2)}, u32[]{:S(2)}) %collective-permute-start.9) | collective-permute-done | bytes 589856 | tf_op jit(solution)/shard_map/ppermute | solution.py:283
  532.0 4.0 collective-permute-start.12
  536.6 4.1 collective-permute-done.10
  540.7 5.4 collective-permute-done.11
  548.2 5.7 %copy.255 = f32[2,750,768]{2,0,1:T(2,128)} copy(f32[2,750,768]{2,1,0:T(8,128)S(1)} %maximum_convert_fusion) | data formatting | bytes 9216000
  (347 shorter events, 171.5 us)
Async XLA Ops:
  7.2 68.4 %copy-start.26 = (bf16[2,750,768]{2,0,1:T(2,128)(2,1)S(1)}, bf16[2,750,768]{2,0,1:T(2,128)(2,1)}, u32[]{:S(2)}) copy-start(bf16[2,750,768]{2,0,1:T(2,128)(2,1)} %param.24) | copy-start | bytes 6912004
  7.2 68.3 %all-gather.3.cloned.1.call-start = ((), (), s32[]{:S(2)}) async-start(), calls=%async_computation | async-start | bytes 2088960 | tf_op jit(solution)/shard_map/all_gather | solution.py:364
  12.6 152.5 %all-gather.5.cloned.1.call-start = ((), (), s32[]{:S(2)}) async-start(), calls=%async_computation.1 | async-start | bytes 5849088 | tf_op jit(solution)/shard_map/all_gather | solution.py:372
  83.6 2.9 collective-permute-start
  86.5 108.9 %copy-start.4 = (bf16[768,768]{1,0:T(8,128)(2,1)}, bf16[768,768]{1,0:T(8,128)(2,1)S(1)}, u32[]{:S(2)}) copy-start(bf16[768,768]{1,0:T(8,128)(2,1)S(1)} %collective-permute-done) | copy-start | bytes 3538948
  87.8 107.6 %copy-start.42 = (f32[1536]{0:T(1024)}, f32[1536]{0:T(1024)S(1)}, u32[]{:S(2)}) copy-start(f32[1536]{0:T(1024)S(1)} %add_rsqrt_fusion.1) | copy-start | bytes 18436
  171.7 21.9 %collective-permute-start.1 = (bf16[1536,768]{1,0:T(8,128)(2,1)}, bf16[1536,768]{1,0:T(8,128)(2,1)}, u32[]{:S(2)}, u32[]{:S(2)}) collective-permute-start(bf16[1536,768]{1,0:T(8,128)(2,1)} %convolution_convert_fusion.1), channel_id=1, source_target_pairs={{0,2},{2,0},{1,3},{3,1},{4,6},{6,4},{5,7},{7,5},{8,10},{10,8},{9,1... | collective-permute-start | bytes 7077896 | tf_op jit(solution)/shard_map/ppermute | solution.py:263
  173.0 58.4 %copy-start.6 = (bf16[768,768]{1,0:T(8,128)(2,1)}, bf16[768,768]{1,0:T(8,128)(2,1)S(1)}, u32[]{:S(2)}) copy-start(bf16[768,768]{1,0:T(8,128)(2,1)S(1)} %pad.8) | copy-start | bytes 3538948
  173.0 5.1 collective-permute-start.2
  237.4 28.3 %collective-permute-start.18 = (bf16[2,4,96,768]{3,2,1,0:T(8,128)(2,1)}, bf16[2,4,96,768]{3,2,1,0:T(8,128)(2,1)}, u32[]{:S(2)}, u32[]{:S(2)}) collective-permute-start(bf16[2,4,96,768]{3,2,1,0:T(8,128)(2,1)} %fusion.34), channel_id=1, source_target_pairs={{0,4},{4,0},{8,12},{12,8},{16,20},{20,16},{24,28},{28,24},{1,5},{5... | collective-permute-start | bytes 3538952 | tf_op jit(solution)/shard_map/ppermute | solution.py:283
  244.9 29.2 %collective-permute-start.13 = (bf16[4,2,96,768]{3,2,1,0:T(8,128)(2,1)}, bf16[4,2,96,768]{3,2,1,0:T(8,128)(2,1)}, u32[]{:S(2)}, u32[]{:S(2)}) collective-permute-start(bf16[4,2,96,768]{3,2,1,0:T(8,128)(2,1)} %fusion.33), channel_id=1, source_target_pairs={{0,1},{1,0},{2,3},{3,2},{4,5},{5,4},{6,7},{7,6},{8,9},{9,8},{10,11... | collective-permute-start | bytes 3538952 | tf_op jit(solution)/shard_map/ppermute | solution.py:276
  247.6 29.6 %collective-permute-start.3 = (bf16[768,768]{1,0:T(8,128)(2,1)}, bf16[768,768]{1,0:T(8,128)(2,1)}, u32[]{:S(2)}, u32[]{:S(2)}) collective-permute-start(bf16[768,768]{1,0:T(8,128)(2,1)} %get-tuple-element.260), channel_id=1, source_target_pairs={{0,2},{2,0},{1,3},{3,1},{4,6},{6,4},{5,7},{7,5},{8,10},{10,8},{9,1... | collective-permute-start | bytes 3538952 | tf_op jit(solution)/shard_map/ppermute | solution.py:263
  254.5 65.0 %collective-permute-start.5 = (bf16[1536,768]{1,0:T(8,128)(2,1)}, bf16[1536,768]{1,0:T(8,128)(2,1)S(1)}, u32[]{:S(2)}, u32[]{:S(2)}) collective-permute-start(bf16[1536,768]{1,0:T(8,128)(2,1)} %get-tuple-element.38), channel_id=1, source_target_pairs={{0,2},{2,0},{1,3},{3,1},{4,6},{6,4},{5,7},{7,5},{8,10},{10,8},{9,1... | collective-permute-start | bytes 7077896 | tf_op jit(solution)/shard_map/ppermute | solution.py:263
  268.2 18.3 %collective-permute-start.19 = (bf16[4,96,768]{2,1,0:T(8,128)(2,1)S(1)}, bf16[4,96,768]{2,1,0:T(8,128)(2,1)S(1)}, u32[]{:S(2)}, u32[]{:S(2)}) collective-permute-start(bf16[4,96,768]{2,1,0:T(8,128)(2,1)S(1)} %fusion.40), channel_id=1, source_target_pairs={{0,1},{1,0},{2,3},{3,2},{4,5},{5,4},{6,7},{7,6},{8,9},{9,8},{10,11... | collective-permute-start | bytes 1769480 | tf_op jit(solution)/shard_map/ppermute | solution.py:276
  276.0 14.8 %collective-permute-start.14 = (bf16[4,96,768]{2,1,0:T(8,128)(2,1)S(1)}, bf16[4,96,768]{2,1,0:T(8,128)(2,1)S(1)}, u32[]{:S(2)}, u32[]{:S(2)}) collective-permute-start(bf16[4,96,768]{2,1,0:T(8,128)(2,1)S(1)} %fusion.39), channel_id=1, source_target_pairs={{0,4},{4,0},{8,12},{12,8},{16,20},{20,16},{24,28},{28,24},{1,5},{5... | collective-permute-start | bytes 1769480 | tf_op jit(solution)/shard_map/ppermute | solution.py:283
  278.8 37.0 %collective-permute-start.4 = (bf16[750,768]{1,0:T(8,128)(2,1)S(1)}, bf16[750,768]{1,0:T(8,128)(2,1)S(1)}, u32[]{:S(2)}, u32[]{:S(2)}) collective-permute-start(bf16[750,768]{1,0:T(8,128)(2,1)S(1)} %fusion.29), channel_id=1, source_target_pairs={{0,1},{1,0},{2,3},{3,2},{4,5},{5,4},{6,7},{7,6},{8,9},{9,8},{10,11... | collective-permute-start | bytes 3456008 | tf_op jit(solution)/shard_map/ppermute | solution.py:417
  286.8 8.7 %collective-permute-start.20 = (bf16[96,768]{1,0:T(8,128)(2,1)S(1)}, bf16[96,768]{1,0:T(8,128)(2,1)S(1)}, u32[]{:S(2)}, u32[]{:S(2)}) collective-permute-start(bf16[96,768]{1,0:T(8,128)(2,1)S(1)} %get-tuple-element.280), channel_id=1, source_target_pairs={{0,8},{4,12},{8,16},{12,20},{16,24},{20,28},{24,0},{28,4},{1,9},{5... | collective-permute-start | bytes 442376 | tf_op jit(solution)/shard_map/ppermute | solution.py:295
  288.0 10.6 %collective-permute-start.22 = (bf16[96,768]{1,0:T(8,128)(2,1)S(1)}, bf16[96,768]{1,0:T(8,128)(2,1)S(1)}, u32[]{:S(2)}, u32[]{:S(2)}) collective-permute-start(bf16[96,768]{1,0:T(8,128)(2,1)S(1)} %get-tuple-element.281), channel_id=1, source_target_pairs={{0,24},{4,28},{8,0},{12,4},{16,8},{20,12},{24,16},{28,20},{1,25},{... | collective-permute-start | bytes 442376 | tf_op jit(solution)/shard_map/ppermute | solution.py:295
  290.8 17.4 %collective-permute-start.21 = (bf16[96,768]{1,0:T(8,128)(2,1)S(1)}, bf16[96,768]{1,0:T(8,128)(2,1)S(1)}, u32[]{:S(2)}, u32[]{:S(2)}) collective-permute-start(bf16[96,768]{1,0:T(8,128)(2,1)S(1)} %get-tuple-element.282), channel_id=1, source_target_pairs={{0,16},{4,20},{8,24},{12,28},{16,0},{20,4},{24,8},{28,12},{1,17},{... | collective-permute-start | bytes 442376 | tf_op jit(solution)/shard_map/ppermute | solution.py:295
  295.5 13.5 %collective-permute-start.15 = (bf16[96,768]{1,0:T(8,128)(2,1)S(1)}, bf16[96,768]{1,0:T(8,128)(2,1)S(1)}, u32[]{:S(2)}, u32[]{:S(2)}) collective-permute-start(bf16[96,768]{1,0:T(8,128)(2,1)S(1)} %get-tuple-element.277), channel_id=1, source_target_pairs={{0,8},{4,12},{8,16},{12,20},{16,24},{20,28},{24,0},{28,4},{1,9},{5... | collective-permute-start | bytes 442376 | tf_op jit(solution)/shard_map/ppermute | solution.py:295
  298.6 10.4 %collective-permute-start.17 = (bf16[96,768]{1,0:T(8,128)(2,1)S(1)}, bf16[96,768]{1,0:T(8,128)(2,1)S(1)}, u32[]{:S(2)}, u32[]{:S(2)}) collective-permute-start(bf16[96,768]{1,0:T(8,128)(2,1)S(1)} %get-tuple-element.278), channel_id=1, source_target_pairs={{0,24},{4,28},{8,0},{12,4},{16,8},{20,12},{24,16},{28,20},{1,25},{... | collective-permute-start | bytes 442376 | tf_op jit(solution)/shard_map/ppermute | solution.py:295
  308.2 6.8 %collective-permute-start.16 = (bf16[96,768]{1,0:T(8,128)(2,1)S(1)}, bf16[96,768]{1,0:T(8,128)(2,1)S(1)}, u32[]{:S(2)}, u32[]{:S(2)}) collective-permute-start(bf16[96,768]{1,0:T(8,128)(2,1)S(1)} %get-tuple-element.279), channel_id=1, source_target_pairs={{0,16},{4,20},{8,24},{12,28},{16,0},{20,4},{24,8},{28,12},{1,17},{... | collective-permute-start | bytes 442376 | tf_op jit(solution)/shard_map/ppermute | solution.py:295
  404.4 40.1 %collective-permute-start.6 = (bf16[768,768]{1,0:T(8,128)(2,1)}, bf16[768,768]{1,0:T(8,128)(2,1)}, u32[]{:S(2)}, u32[]{:S(2)}) collective-permute-start(bf16[768,768]{1,0:T(8,128)(2,1)} %slice.212), channel_id=1, source_target_pairs={{0,2},{2,0},{1,3},{3,1},{4,6},{6,4},{5,7},{7,5},{8,10},{10,8},{9,1... | collective-permute-start | bytes 3538952 | tf_op jit(solution)/shard_map/ppermute | solution.py:263
  443.6 73.2 %collective-permute-start.8 = (bf16[4,2,96,768]{3,2,1,0:T(8,128)(2,1)}, bf16[4,2,96,768]{3,2,1,0:T(8,128)(2,1)S(1)}, u32[]{:S(2)}, u32[]{:S(2)}) collective-permute-start(bf16[4,2,96,768]{3,2,1,0:T(8,128)(2,1)} %copy.247), channel_id=1, source_target_pairs={{0,1},{1,0},{2,3},{3,2},{4,5},{5,4},{6,7},{7,6},{8,9},{9,8},{10,11... | collective-permute-start | bytes 3538952 | tf_op jit(solution)/shard_map/ppermute | solution.py:276
  444.5 72.2 %copy-start.13 = (f32[1,4,2,96,768]{4,3,2,1,0:T(8,128)S(1)}, f32[1,4,2,96,768]{4,3,2,1,0:T(8,128)}, u32[]{:S(2)}) copy-start(f32[1,4,2,96,768]{4,3,2,1,0:T(8,128)} %copy.246) | copy-start | bytes 7077892
  517.1 14.6 %collective-permute-start.9 = (bf16[4,96,768]{2,1,0:T(8,128)(2,1)S(1)}, bf16[4,96,768]{2,1,0:T(8,128)(2,1)S(1)}, u32[]{:S(2)}, u32[]{:S(2)}) collective-permute-start(bf16[4,96,768]{2,1,0:T(8,128)(2,1)S(1)} %fusion.38), channel_id=1, source_target_pairs={{0,4},{4,0},{8,12},{12,8},{16,20},{20,16},{24,28},{28,24},{1,5},{5... | collective-permute-start | bytes 1769480 | tf_op jit(solution)/shard_map/ppermute | solution.py:283
  520.4 27.3 %collective-permute-start.7 = (bf16[750,768]{1,0:T(8,128)(2,1)S(1)}, bf16[750,768]{1,0:T(8,128)(2,1)S(1)}, u32[]{:S(2)}, u32[]{:S(2)}) collective-permute-start(bf16[750,768]{1,0:T(8,128)(2,1)S(1)} %fusion.24), channel_id=1, source_target_pairs={{0,1},{1,0},{2,3},{3,2},{4,5},{5,4},{6,7},{7,6},{8,9},{9,8},{10,11... | collective-permute-start | bytes 3456008 | tf_op jit(solution)/shard_map/ppermute | solution.py:437
  524.1 22.0 %copy-start.23 = (f32[96,768]{1,0:T(8,128)S(1)}, f32[96,768]{1,0:T(8,128)}, u32[]{:S(2)}) copy-start(f32[96,768]{1,0:T(8,128)} %fusion.45) | copy-start | bytes 884740
  532.0 8.7 %collective-permute-start.10 = (bf16[96,768]{1,0:T(8,128)(2,1)S(1)}, bf16[96,768]{1,0:T(8,128)(2,1)S(1)}, u32[]{:S(2)}, u32[]{:S(2)}) collective-permute-start(bf16[96,768]{1,0:T(8,128)(2,1)S(1)} %get-tuple-element.283), channel_id=1, source_target_pairs={{0,8},{4,12},{8,16},{12,20},{16,24},{20,28},{24,0},{28,4},{1,9},{5... | collective-permute-start | bytes 442376 | tf_op jit(solution)/shard_map/ppermute | solution.py:295
  532.0 8.7 %collective-permute-start.12 = (bf16[96,768]{1,0:T(8,128)(2,1)S(1)}, bf16[96,768]{1,0:T(8,128)(2,1)S(1)}, u32[]{:S(2)}, u32[]{:S(2)}) collective-permute-start(bf16[96,768]{1,0:T(8,128)(2,1)S(1)} %get-tuple-element.284), channel_id=1, source_target_pairs={{0,24},{4,28},{8,0},{12,4},{16,8},{20,12},{24,16},{28,20},{1,25},{... | collective-permute-start | bytes 442376 | tf_op jit(solution)/shard_map/ppermute | solution.py:295
  536.0 10.1 %collective-permute-start.11 = (bf16[96,768]{1,0:T(8,128)(2,1)S(1)}, bf16[96,768]{1,0:T(8,128)(2,1)S(1)}, u32[]{:S(2)}, u32[]{:S(2)}) collective-permute-start(bf16[96,768]{1,0:T(8,128)(2,1)S(1)} %get-tuple-element.285), channel_id=1, source_target_pairs={{0,16},{4,20},{8,24},{12,28},{16,0},{20,4},{24,8},{28,12},{1,17},{... | collective-permute-start | bytes 442376 | tf_op jit(solution)/shard_map/ppermute | solution.py:295
  546.2 7.7 %collective-permute-start.23 = (f32[96,2304]{1,0:T(8,128)S(1)}, f32[96,2304]{1,0:T(8,128)S(1)}, u32[]{:S(2)}, u32[]{:S(2)}) collective-permute-start(f32[96,2304]{1,0:T(8,128)S(1)} %pad_maximum_fusion.3), channel_id=1, source_target_pairs={{0,2},{2,0},{1,3},{3,1},{4,6},{6,4},{5,7},{7,5},{8,10},{10,8},{9,1... | collective-permute-start | bytes 2654216 | tf_op jit(solution)/shard_map/ppermute | solution.py:263
  (63 other events, 348.3 us)
Sparse Core Ops, SparseCore 0:
  12.7 62.7 all-gather.2
  78.9 86.1 all-gather.4
